TPU v7x, 1024 devices: a whole 4x8x16 slice. The times are simulated.
1024 devices in a mesh: leaf: 128 (over x, z, core), grp: 8 (over y).
Axes of the slice: x: 4, y: 8, z: 16, core: 2. Of those that a mesh axis runs over, the one named last changes fastest.
Arguments:
- charges: bfloat16 [64, 2097152], P(None, ('leaf', 'grp')), may hold values from -6 to 6
- positions: bfloat16 [3, 2097152], P(None, ('leaf', 'grp')), may hold values from 0 to 1
- bases: bfloat16 [64, 2097152], P(None, ('leaf', 'grp')), may hold values from -0.5 to 0.5
- transfers: bfloat16 [16384, 64, 64], P(('leaf', 'grp')), may hold values from -0.1875 to 0.1875
- couplings: bfloat16 [128, 4096, 64], P('leaf', 'grp'), may hold values from -0.09375 to 0.09375
- far_source: int32 [128, 64], P('leaf'), may hold values from 0 to 127, as said below
- wanted: int32 [128, 8, 8, 8], P('leaf', 'grp'), may hold values from 0 to 15, as said below
- near_target: int32 [128, 8, 512], P('leaf', 'grp'), may hold values from 0 to 15
- near_slot: int32 [128, 8, 512], P('leaf', 'grp'), may hold values from 0 to 63, as said below
Outputs:
- potential: bfloat16 [64, 2097152], P(None, ('leaf', 'grp'))
Inputs may be any that keep to these rules, and one draw needn't show every extreme that they name: `far_source`: the entries of one target's list are distinct and never the target itself. wanted[i, g, h, c] is a leaf numbered within device (i, h); the 8 entries of one [i, g, h] are distinct. `near_slot`: the value h * 8 + c names slot c of group device h.
All inputs are finite; a program needn't handle non-finite values.
Results may differ from a plain program's by a relative error of at most 0.007.
Values may be sent and summed in bfloat16 or wider, within the bound.
A program may use at most 32 MiB of HBM per device.

v0:
```python
import jax
import jax.numpy as jnp
from jax import lax
from jax.sharding import PartitionSpec as P

soften = 0.05


def near_field(target_pos, source_rows, source_pos, target_list, source_list, leaves, leaf_size):
    rhs_count = source_rows.shape[0]
    batch_size = 16
    step_count = target_list.shape[0] // batch_size
    target_batches = target_list.reshape(step_count, batch_size)
    source_batches = source_list.reshape(step_count, batch_size)

    def add_batch(total, lists):
        target_ids, source_ids = lists
        target_here = jnp.take(target_pos, target_ids, axis=1)
        source_here = jnp.take(source_pos, source_ids, axis=1)
        offset = target_here[:, :, :, None] - source_here[:, :, None, :]
        squared = jnp.sum(offset * offset, axis=0)
        block = (1.0 / (leaf_size * jnp.sqrt(squared + soften * soften))).astype(jnp.bfloat16)
        picked_rows = jnp.take(source_rows, source_ids, axis=1)
        contribution = jnp.einsum(
            "rjb,jab->jra", picked_rows, block, preferred_element_type=jnp.float32
        )
        placement = (target_ids[:, None] == jnp.arange(leaves)[None, :]).astype(jnp.float32)
        total = total + jnp.einsum(
            "jl,jra->rla", placement, contribution, precision=lax.Precision.HIGHEST
        )
        return (total, None)

    start = jnp.zeros((rhs_count, leaves, leaf_size), jnp.float32)
    near_part, _ = lax.scan(add_batch, start, (target_batches, source_batches))
    return near_part


def shards(
    charges, positions, bases, transfers, couplings, far_source, wanted, near_target, near_slot
):
    rhs_count, local_points = charges.shape
    rank_size = bases.shape[0]
    leaves = transfers.shape[0]
    leaf_size = local_points // leaves
    slot_cap = wanted.shape[-1]
    per_device = couplings.shape[1] // rank_size
    charge_leaf = charges.reshape(rhs_count, leaves, leaf_size)
    pos_leaf = positions.reshape(3, leaves, leaf_size)
    basis_leaf = bases.reshape(rank_size, leaves, leaf_size)
    leaf_coeff = jnp.einsum(
        "kln,rln->lkr", basis_leaf, charge_leaf, preferred_element_type=jnp.float32
    ).astype(jnp.bfloat16)
    partial_value = jnp.einsum(
        "lab,lbr->ar", transfers, leaf_coeff, preferred_element_type=jnp.float32
    )
    own_panels = couplings.reshape(per_device, rank_size, rank_size)
    far_list = far_source[0]
    cluster_coeff = lax.psum(partial_value, "grp").astype(jnp.bfloat16)
    all_coeffs = lax.all_gather(cluster_coeff[None], "leaf", axis=0, tiled=True)
    own_list = lax.dynamic_slice_in_dim(far_list, lax.axis_index("grp") * per_device, per_device)
    selected_entries = jnp.take(all_coeffs, own_list, axis=0)
    target_part = jnp.einsum(
        "jab,jbr->ar", own_panels, selected_entries, preferred_element_type=jnp.float32
    )
    target_coefficient = lax.psum(target_part, "grp").astype(jnp.bfloat16)
    leaf_of_target = jnp.einsum(
        "lab,ar->lbr", transfers, target_coefficient, preferred_element_type=jnp.float32
    ).astype(jnp.bfloat16)
    far_part = jnp.einsum(
        "kln,lkr->rln", basis_leaf, leaf_of_target, preferred_element_type=jnp.float32
    )
    request_table = wanted[0, 0]
    slot_ids = near_slot[0, 0]
    target_list = near_target[0, 0]
    source_rows, source_pos = (
        lax.all_gather(charge_leaf, "grp", axis=1, tiled=True),
        lax.all_gather(pos_leaf, "grp", axis=1, tiled=True),
    )
    flat_table = request_table.reshape(-1)
    source_list = jnp.take(flat_table, slot_ids) + slot_ids // slot_cap * leaves
    near_part = near_field(
        pos_leaf.astype(jnp.float32),
        source_rows,
        source_pos.astype(jnp.float32),
        target_list,
        source_list,
        leaves,
        leaf_size,
    )
    potential = (near_part + far_part).astype(jnp.bfloat16)
    return potential.reshape(rhs_count, local_points)


def solution(mesh):
    in_specs = (
        P(None, ("leaf", "grp")),
        P(None, ("leaf", "grp")),
        P(None, ("leaf", "grp")),
        P(("leaf", "grp"), None, None),
        P("leaf", "grp", None),
        P("leaf", None),
        P("leaf", "grp", None, None),
        P("leaf", "grp", None),
        P("leaf", "grp", None),
    )
    out_specs = P(None, ("leaf", "grp"))
    return jax.shard_map(shards, mesh=mesh, in_specs=in_specs, out_specs=out_specs, check_vma=False)
```

profile of v0, /device:TPU:1, one launch (start us, length us, event | category | flops | bytes accessed | tf_op | source)
XLA Modules:
  0.0 449.6 jit_solution(13425886947070617972)
XLA Ops:
  7.5 1.5 fusion.22
  9.0 24.0 %psum.14 = bf16[64,64]{0,1:T(8,128)(2,1)S(1)} all-reduce(f32[64,64]{0,1:T(8,128)S(1)} %fusion.22), channel_id=1, replica_groups=mesh['leaf'=128,'grp'=8] {'grp'}, use_global_device_ids=true, to_apply=%region_3.4 | all-reduce | flops 4096 | bytes 24576 | tf_op jit(solution)/shard_map/psum | solution.py:58
  33.8 1.7 copy.72
  39.2 5.1 %compare_select_fusion.5 = (s32[512,1]{0,1:T(1,128)S(1)}, s32[512,1]{0,1:T(1,128)S(1)}) fusion(s32[]{:T(128)} %bitcast.58, s32[]{:T(128)} %bitcast.59, s32[]{:T(128)} %bitcast.60, s32[]{:T(128)} %bitcast.61, s32[]{:T(128)} %bitcast.62, s32[]{:T(128)} %bitcast.64, s32[]{:T(128)} %bitcast.63, s32[1,1,512]{2,1,0:T(1,128)} %param.19), kind=kLoop, calls=%fused_computation.127 | loop fusion | flops 7680 | bytes 6172 | tf_op jit(solution)/shard_map/jit(_take)/gather | solution.py:80
  44.7 35.6 %select_select_fusion = s32[512]{0:T(512)S(1)} fusion(pred[512]{0:T(512)(128)(4,1)S(1)} %get-tuple-element.144, pred[512]{0:T(512)(128)(4,1)S(1)} %get-tuple-element.143, pred[512]{0:T(512)(128)(4,1)S(1)} %get-tuple-element.142, pred[512]{0:T(512)(128)(4,1)S(1)} %get-tuple-element.141, pred[512]{0:T(512)(128)(4,1)S(1)} %get-tuple-element.140, ...), kind=kLoop, calls=%fused_computation.136 | loop fusion | flops 29184 | bytes 33508 | tf_op jit(solution)/shard_map/jit(_take)/gather | solution.py:80
  81.8 19.4 %all_gather.10 = bf16[3,128,128]{2,1,0:T(8,128)(2,1)S(1)} all-gather(bf16[3,16,128]{2,1,0:T(8,128)(2,1)S(1)} %bitcast.184), channel_id=1, replica_groups=mesh['leaf'=128,'grp'=8] {'grp'}, dimensions={1}, use_global_device_ids=true | all-gather | bytes 110592 | tf_op jit(solution)/shard_map/all_gather | solution.py:77
  102.4 90.8 %all-gather.6.cloned.1.call-done = bf16[8192,64]{1,0:T(8,128)(2,1)} async-done(((bf16[64,64]{1,0:T(8,128)(2,1)}), bf16[8192,64]{1,0:T(8,128)(2,1)}) %all-gather.6.cloned.1.call-update) | async-done | bytes 1048592 | tf_op jit(solution)/shard_map/all_gather | solution.py:59
  193.2 2.2 gather_fusion.3
  195.7 23.2 %psum.15 = bf16[64,64]{0,1:T(8,128)(2,1)S(1)} all-reduce(f32[64,64]{0,1:T(8,128)S(1)} %convolution_bitcast_fusion.2), channel_id=1, replica_groups=mesh['leaf'=128,'grp'=8] {'grp'}, use_global_device_ids=true, to_apply=%region_4.5 | all-reduce | flops 4096 | bytes 24576 | tf_op jit(solution)/shard_map/psum | solution.py:65
  218.9 23.8 %all-gather.4.cloned.1.call-done = bf16[64,128,128]{2,1,0:T(8,128)(2,1)} async-done(((bf16[64,16,128]{2,1,0:T(8,128)(2,1)}), bf16[64,128,128]{2,1,0:T(8,128)(2,1)}) %all-gather.4.cloned.1.call-update) | async-done | bytes 2097168 | tf_op jit(solution)/shard_map/all_gather | solution.py:76
  242.7 4.2 copy.51
  247.0 194.7 %while.11 = (s32[]{:T(128)}, f32[64,16,128]{2,1,0:T(8,128)S(1)}, s32[32,16]{1,0:T(8,128)S(1)}, bf16[64,128,128]{2,0,1:T(8,128)(2,1)}, s32[32,16]{1,0:T(8,128)S(1...) while((s32[]{:T(128)}, f32[64,16,128]{2,1,0:T(8,128)S(1)}, ...), condition=%wide.region_2.3_spmd.clone, body=%wide.region_0.2_spmd.clone.sunk | while | flops 62274080 | bytes 5334015 | solution.py:34
  248.4 1.0 multiply_reduce_fusion.2
  249.4 2.2 gather_fusion.2
  254.5 1.0 multiply_reduce_fusion.2
  255.5 2.2 gather_fusion.2
  260.6 1.0 multiply_reduce_fusion.2
  261.6 2.2 gather_fusion.2
  266.7 1.0 multiply_reduce_fusion.2
  267.7 2.2 gather_fusion.2
  272.7 1.0 multiply_reduce_fusion.2
  273.8 2.2 gather_fusion.2
  278.8 1.0 multiply_reduce_fusion.2
  279.9 2.2 gather_fusion.2
  284.9 1.0 multiply_reduce_fusion.2
  286.0 2.2 gather_fusion.2
  291.0 1.0 multiply_reduce_fusion.2
  292.0 2.2 gather_fusion.2
  297.1 1.0 multiply_reduce_fusion.2
  298.1 2.2 gather_fusion.2
  303.2 1.0 multiply_reduce_fusion.2
  304.2 2.2 gather_fusion.2
  309.2 1.0 multiply_reduce_fusion.2
  310.3 2.2 gather_fusion.2
  315.3 1.0 multiply_reduce_fusion.2
  316.4 2.2 gather_fusion.2
  321.4 1.0 multiply_reduce_fusion.2
  322.5 2.2 gather_fusion.2
  327.5 1.0 multiply_reduce_fusion.2
  328.5 2.2 gather_fusion.2
  333.6 1.0 multiply_reduce_fusion.2
  334.6 2.2 gather_fusion.2
  339.7 1.0 multiply_reduce_fusion.2
  340.7 2.2 gather_fusion.2
  345.7 1.0 multiply_reduce_fusion.2
  346.8 2.2 gather_fusion.2
  352.9 2.2 gather_fusion.2
  359.0 2.2 gather_fusion.2
  365.0 2.2 gather_fusion.2
  371.1 2.2 gather_fusion.2
  377.2 2.2 gather_fusion.2
  383.3 2.2 gather_fusion.2
  389.4 2.2 gather_fusion.2
  394.4 1.0 multiply_reduce_fusion.2
  395.5 2.2 gather_fusion.2
  401.5 2.2 gather_fusion.2
  406.6 1.0 multiply_reduce_fusion.2
  407.6 2.2 gather_fusion.2
  413.7 2.2 gather_fusion.2
  419.8 2.2 gather_fusion.2
  425.9 2.2 gather_fusion.2
  432.0 2.2 gather_fusion.2
  437.0 1.0 multiply_reduce_fusion.2
  438.0 2.2 gather_fusion.2
  (439 shorter events, 110.4 us)
Async XLA Ops:
  6.5 1.0 copy-start
  6.5 74.4 %copy-start.4 = (s32[1,1,512]{2,1,0:T(1,128)S(1)}, s32[1,1,512]{2,1,0:T(1,128)}, u32[]{:S(2)}) copy-start(s32[1,1,512]{2,1,0:T(1,128)} %param.19) | copy-start | bytes 6148
  6.5 75.2 %copy-start.3 = (bf16[3,2048]{1,0:T(4,128)(2,1)S(1)}, bf16[3,2048]{1,0:T(4,128)(2,1)}, u32[]{:S(2)}) copy-start(bf16[3,2048]{1,0:T(4,128)(2,1)} %param.12) | copy-start | bytes 36868
  6.5 94.7 %copy-start.5 = (s32[1,1,512]{2,1,0:T(1,128)S(1)}, s32[1,1,512]{2,1,0:T(1,128)}, u32[]{:S(2)}) copy-start(s32[1,1,512]{2,1,0:T(1,128)} %param.18) | copy-start | bytes 6148
  6.5 95.5 %copy-start.2 = (bf16[1,512,64]{1,2,0:T(8,128)(2,1)S(1)}, bf16[1,512,64]{1,2,0:T(8,128)(2,1)}, u32[]{:S(2)}) copy-start(bf16[1,512,64]{1,2,0:T(8,128)(2,1)} %param.15) | copy-start | bytes 196612
  6.5 95.7 %copy-start.6 = (s32[1,64]{1,0:T(1,128)S(1)}, s32[1,64]{1,0:T(1,128)}, u32[]{:S(2)}) copy-start(s32[1,64]{1,0:T(1,128)} %param.16) | copy-start | bytes 772
  6.6 186.7 %all-gather.6.cloned.1.call-start = ((), (), s32[]{:S(2)}) async-start(), calls=%async_computation.1 | async-start | bytes 2113536 | tf_op jit(solution)/shard_map/all_gather | solution.py:59
  33.7 209.0 %all-gather.4.cloned.1.call-start = ((), (), s32[]{:S(2)}) async-start(), calls=%async_computation | async-start | bytes 2359296 | tf_op jit(solution)/shard_map/all_gather | solution.py:76
  247.0 194.7 %copy-start.1 = (bf16[64,2048]{1,0:T(8,128)(2,1)S(1)}, bf16[64,2048]{1,0:T(8,128)(2,1)}, u32[]{:S(2)}) copy-start(bf16[64,2048]{1,0:T(8,128)(2,1)} %param.13) | copy-start | bytes 786436
Sparse Core Ops, SparseCore 0:
  33.8 159.3 all-gather.5
  195.8 46.8 all-gather.3
where the time goes:
time: 455 us; the launch traced here: 450 us
  local copies, waits for them, and re-layouts  123 us (27%)
  waiting for transfers between devices  115 us (25%)
  other arithmetic  82.5 us (18%)
  blocking collectives  66.6 us (15%)
  matrix products  45.9 us (10%)
  between operations  13.6 us (3%)
    all_gather x1, waiting for transfers between devices, shards(): all_coeffs = lax.all_gather(cluster_coeff[None], 'leaf', axis=0, tiled=True)  90.8 us
    gather x32, local copies, waits for them, and re-layouts, add_batch(): picked_rows = jnp.take(source_rows, source_ids, axis=1)  70 us
    gather x3, other arithmetic, shards(): source_list = jnp.take(flat_table, slot_ids) + slot_ids // slot_cap * leaves  41.1 us
    reduce_sum x32, other arithmetic, add_batch(): squared = jnp.sum(offset * offset, axis=0)  33.3 us
    dot_general x32, matrix products, add_batch(): jnp.einsum('jl,jra->rla', placement, contribution, precision=lax.Precisio...  26.1 us
    psum x1, blocking collectives, shards(): cluster_coeff = lax.psum(partial_value, 'grp').astype(jnp.bfloat16)  24 us
    all_gather x1, waiting for transfers between devices, shards(): lax.all_gather(charge_leaf, 'grp', axis=1, tiled=True)  23.8 us
    psum x1, blocking collectives, shards(): target_coefficient = lax.psum(target_part, 'grp').astype(jnp.bfloat16)  23.2 us
  transfers between devices with their start and end apart: 2, of which 2 were waited for; matrix products, arithmetic and copies ran while one was open for 11% of the time, Pallas kernels for 0%

commit v1 on v0

v1 whole, which is shorter than its diff:
```python
import functools

import jax
import jax.numpy as jnp
from jax import lax
from jax.experimental import pallas as pl
from jax.experimental.pallas import tpu as pltpu
from jax.sharding import PartitionSpec as P

MESH = pl.DeviceIdType.MESH
bf = jnp.bfloat16
f32 = jnp.float32
GRP = 8
LEAVES = 16
BS = 128
CAP = 8
HALF = LEAVES // 2
FEATS = 16
SOFTEN2 = 0.05 * 0.05
SCALE = float(BS * BS)
NT = (((1,), (1,)), ((), ()))


def dot_nt(a, b):
    return lax.dot_general(a, b, NT, preferred_element_type=f32)


def dot(a, b):
    return jnp.dot(a, b, preferred_element_type=f32)


def pack(x):
    return jnp.concatenate([x[:32, :], x[32:, :]], axis=1)


def unpack(x):
    return jnp.concatenate([x[:, :64], x[:, 64:]], axis=0)


def pieces(n):
    high = n.astype(bf).astype(f32)
    rest = n - high
    middle = rest.astype(bf).astype(f32)
    return high, middle, rest - middle


def kernel(
    dims,
    wanted,
    far_source,
    charges,
    positions,
    bases,
    transfers,
    couplings,
    near_target,
    near_slot,
    out,
    ch0,
    ch1,
    ch2,
    ch3,
    ch4,
    ch5,
    ch6,
    ch7,
    ps0,
    ps1,
    ps2,
    ps3,
    ps4,
    ps5,
    ps6,
    ps7,
    pos_rows,
    target_feat,
    source_feat,
    feat_sel,
    feat_sel_t,
    charge_sel,
    weight,
    acc,
    part_up,
    part_down,
    coeffs,
    ring_send,
    ring_recv,
    pos_send,
    pos_recv,
    up_send,
    up_recv,
    down_send,
    down_recv,
    z_send,
    z_recv,
    x_send,
    x_recv,
    core_send,
    core_recv,
):
    X, Z, C = dims
    leaf = lax.axis_index("leaf")
    y = lax.axis_index("grp")
    x = leaf // (Z * C)
    z = (leaf // C) % Z
    core = leaf % C
    chunk = [ch0, ch1, ch2, ch3, ch4, ch5, ch6, ch7]
    place = [ps0, ps1, ps2, ps3, ps4, ps5, ps6, ps7]

    def y_peer(k):
        return (leaf, (y + k) % GRP)

    def z_peer(k):
        return ((x * Z + (z + k) % Z) * C + core, y)

    def x_peer(k):
        return ((((x + k) % X) * Z + z) * C + core, y)

    core_peer = ((x * Z + z) * C + (1 - core), y)

    barrier = pltpu.get_barrier_semaphore()

    def greet(peer):
        pl.semaphore_signal(barrier, inc=1, device_id=peer, device_id_type=MESH)

    for k in range(1, GRP):
        greet(y_peer(k))
    for k in range(1, Z):
        greet(z_peer(k))
    for k in range(1, X):
        greet(x_peer(k))
    if C > 1:
        greet(core_peer)

    pos = positions[...].astype(f32)
    for d in range(3):
        for t in range(LEAVES):
            row = d * LEAVES + t
            pos_rows[row : row + 1, :] = pos[d : d + 1, t * BS : (t + 1) * BS]
    ps0[...] = pos_rows[...].astype(bf)
    for t in range(LEAVES):
        ch0[t] = charges[:, t * BS : (t + 1) * BS]

    partial = None
    for t in range(LEAVES):
        cols = slice(t * BS, (t + 1) * BS)
        leaf_coeff = dot_nt(charges[:, cols], bases[:, cols]).astype(bf)
        term = dot_nt(leaf_coeff, transfers[t])
        partial = term if partial is None else partial + term
    part_up[0] = pack(partial).astype(bf)

    pl.semaphore_wait(barrier, (GRP - 1) + (Z - 1) + (X - 1) + (C - 1))

    def exchange(buf, send, recv, k):
        return pltpu.make_async_remote_copy(
            src_ref=buf.at[0],
            dst_ref=buf.at[k],
            send_sem=send.at[k],
            recv_sem=recv.at[k],
            device_id=y_peer(k),
            device_id_type=MESH,
        )

    def ring(right, step, half):
        src = step if right else (GRP - step) % GRP
        dst = step + 1 if right else GRP - step - 1
        part = pl.ds(half * HALF, HALF)
        way = 0 if right else 1
        slot = 2 * step + (half if step < 3 else 0)
        return pltpu.make_async_remote_copy(
            src_ref=chunk[src].at[part],
            dst_ref=chunk[dst].at[part],
            send_sem=ring_send.at[way, slot],
            recv_sem=ring_recv.at[way, slot],
            device_id=y_peer(1 if right else GRP - 1),
            device_id_type=MESH,
        )

    def ring_pos(right, step):
        src = step if right else (GRP - step) % GRP
        dst = step + 1 if right else GRP - step - 1
        way = 0 if right else 1
        return pltpu.make_async_remote_copy(
            src_ref=place[src],
            dst_ref=place[dst],
            send_sem=pos_send.at[way, step],
            recv_sem=pos_recv.at[way, step],
            device_id=y_peer(1 if right else GRP - 1),
            device_id_type=MESH,
        )

    def slot_of(x_at, z_at):
        return (core * X + x_at) * Z + z_at

    def z_copy(k, z_at):
        here = coeffs.at[slot_of(x, z_at)]
        return pltpu.make_async_remote_copy(
            src_ref=here,
            dst_ref=here,
            send_sem=z_send.at[k],
            recv_sem=z_recv.at[k],
            device_id=z_peer(k),
            device_id_type=MESH,
        )

    def x_copy(k, x_at):
        here = coeffs.at[pl.ds(slot_of(x_at, 0), Z)]
        return pltpu.make_async_remote_copy(
            src_ref=here,
            dst_ref=here,
            send_sem=x_send.at[k],
            recv_sem=x_recv.at[k],
            device_id=x_peer(k),
            device_id_type=MESH,
        )

    def core_copy(core_at):
        here = coeffs.at[pl.ds(core_at * (X * Z), X * Z)]
        return pltpu.make_async_remote_copy(
            src_ref=here,
            dst_ref=here,
            send_sem=core_send,
            recv_sem=core_recv,
            device_id=core_peer,
            device_id_type=MESH,
        )

    for k in range(1, GRP):
        exchange(part_up, up_send, up_recv, k).start()
    for right in (True, False):
        ring_pos(right, 0).start()
    for half in (0, 1):
        for right in (True, False):
            ring(right, 0, half).start()

    norm = jnp.sum(pos * pos, axis=0, keepdims=True) + SOFTEN2
    high, middle, low = pieces(norm)
    one = jnp.ones_like(norm)
    target_feat[...] = (
        jnp.concatenate(
            [-2.0 * pos, high, middle, low, one, one, one, jnp.zeros((FEATS - 9, norm.shape[1]), f32)],
            axis=0,
        )
        * SCALE
    ).astype(bf)
    source_feat[...] = jnp.zeros_like(source_feat)
    for f in (3, 4, 5):
        source_feat[:, f, :] = jnp.ones((LEAVES, BS), f32)

    blocks = near_slot.shape[1]
    slot_hot = (
        lax.broadcasted_iota(jnp.int32, (GRP * CAP, blocks), 0) == near_slot[...]
    ).astype(f32)
    leaf_hot = (
        lax.broadcasted_iota(jnp.int32, (LEAVES, blocks), 0) == near_target[...]
    ).astype(f32)
    counts = dot_nt(slot_hot.astype(bf), leaf_hot.astype(bf))
    spread = (
        lax.broadcasted_iota(jnp.int32, (LEAVES, LEAVES * BS), 1) // BS
        == lax.broadcasted_iota(jnp.int32, (LEAVES, LEAVES * BS), 0)
    ).astype(f32)
    spread_counts = dot(counts.astype(bf), spread.astype(bf))
    for h in range(GRP):
        weight[h] = spread_counts[h * CAP : (h + 1) * CAP, :]

    def near(rel, first=False, last=False):
        h = (y + (GRP - rel)) % GRP
        rows = place[rel][...].astype(f32)
        px, py, pz = rows[0:16], rows[16:32], rows[32:48]
        parts = pieces(px * px + py * py + pz * pz)
        for f, v in zip((0, 1, 2, 6, 7, 8), (px, py, pz) + parts):
            source_feat[:, f, :] = v
        for c in range(CAP):
            at = wanted[h, c]
            cols = slice(c * BS, (c + 1) * BS)
            charge_sel[:, cols] = chunk[rel][at]
            feat_sel[:, cols] = source_feat[at]
        feat_sel_t[...] = feat_sel[...].T.astype(bf)
        width, depth = 1024, 512

        def block(i, carry):
            cols = pl.ds(pl.multiple_of(i * width, width), width)
            targets = target_feat[:, cols]
            w = weight[h, :, cols].astype(bf)
            total = None
            for k in range(0, CAP * BS, depth):
                dist = dot(feat_sel_t[k : k + depth, :], targets)
                g = lax.rsqrt(dist.astype(bf))
                g = jnp.concatenate(
                    [
                        g[j * BS : (j + 1) * BS, :] * w[k // BS + j : k // BS + j + 1, :]
                        for j in range(depth // BS)
                    ],
                    axis=0,
                )
                term = dot(charge_sel[:, k : k + depth], g)
                total = term if total is None else total + term
            if not first:
                total = total + acc[:, cols]
            if last:
                out[:, cols] = total.astype(bf)
            else:
                acc[:, cols] = total
            return carry

        lax.fori_loop(0, LEAVES * BS // width, block, 0)

    def arrived(step, half, right=True, left=True):
        for way in (True, False):
            if (right if way else left):
                if half == 0 or step == 3:
                    if not (step == 3 and not way):
                        ring_pos(way, step).wait_recv()
                        if step < 2 or (step == 2 and way):
                            ring_pos(way, step + 1).start()
                ring(way, step, half).wait_recv()
                if step < 2:
                    ring(way, step + 1, half).start()
                elif step == 2 and (half == 0) == way:
                    ring(way, 3, half).start()

    near(0, first=True)
    arrived(0, 0)

    for k in range(1, GRP):
        exchange(part_up, up_send, up_recv, k).wait_recv()
    total = part_up[0].astype(f32)
    for k in range(1, GRP):
        total = total + part_up[k].astype(f32)
    coeffs[slot_of(x, z)] = total.astype(bf)
    for k in range(1, Z):
        z_copy(k, z).start()

    arrived(0, 1)
    near(1)
    for k in range(1, Z):
        z_copy(k, (z + (Z - k)) % Z).wait_recv()
    for k in range(1, X):
        x_copy(k, x).start()
    arrived(1, 0)
    near(7)
    for k in range(1, X):
        x_copy(k, (x + (X - k)) % X).wait_recv()
    if C > 1:
        core_copy(core).start()
    arrived(1, 1)
    near(2)
    arrived(2, 0)
    near(6)
    if C > 1:
        core_copy(1 - core).wait_recv()

    partial = None
    rank = couplings.shape[1]
    for j in range(couplings.shape[0] // rank):
        source = far_source[0, y * (couplings.shape[0] // rank) + j]
        slot = source if C == 1 else (source & 1) * (X * Z) + (source >> 1)
        term = dot_nt(unpack(coeffs[slot]), couplings[j * rank : (j + 1) * rank, :])
        partial = term if partial is None else partial + term
    part_down[0] = pack(partial).astype(bf)
    for k in range(1, GRP):
        exchange(part_down, down_send, down_recv, k).start()

    arrived(2, 1)
    near(3)

    for k in range(1, GRP):
        exchange(part_down, down_send, down_recv, k).wait_recv()
    total = part_down[0].astype(f32)
    for k in range(1, GRP):
        total = total + part_down[k].astype(f32)
    target_coeff = unpack(total.astype(bf))
    for t in range(LEAVES):
        cols = slice(t * BS, (t + 1) * BS)
        leaf_target = dot(target_coeff, transfers[t]).astype(bf)
        acc[:, cols] += dot(leaf_target, bases[:, cols])

    near(5)
    arrived(3, 0, left=False)
    arrived(3, 1, right=False)
    near(4, last=True)

    for k in range(1, GRP):
        exchange(part_up, up_send, up_recv, k).wait_send()
        exchange(part_down, down_send, down_recv, k).wait_send()
    for right in (True, False):
        for step in range(3):
            ring_pos(right, step).wait_send()
            for half in (0, 1):
                ring(right, step, half).wait_send()
    ring_pos(True, 3).wait_send()
    ring(True, 3, 0).wait_send()
    ring(False, 3, 1).wait_send()
    for k in range(1, Z):
        z_copy(k, z).wait_send()
    for k in range(1, X):
        x_copy(k, x).wait_send()
    if C > 1:
        core_copy(core).wait_send()


def solution(mesh):
    n_leaf = mesh.shape["leaf"]
    dims = {128: (4, 16, 2), 1: (1, 1, 1), 2: (1, 1, 2), 8: (2, 2, 2), 16: (2, 4, 2)}[n_leaf]
    X, Z, C = dims

    def shards(charges, positions, bases, transfers, couplings, far_source, wanted, near_target, near_slot):
        vmem = pl.BlockSpec(memory_space=pltpu.VMEM)
        smem = pl.BlockSpec(memory_space=pltpu.SMEM)
        rows, points = charges.shape
        dma = pltpu.SemaphoreType.DMA
        return pl.pallas_call(
            functools.partial(kernel, dims),
            out_shape=jax.ShapeDtypeStruct(charges.shape, bf),
            in_specs=[smem, smem] + [vmem] * 7,
            out_specs=vmem,
            scratch_shapes=[pltpu.VMEM((LEAVES, rows, BS), bf)] * 8
            + [pltpu.VMEM((3 * LEAVES, BS), bf)] * 8
            + [
                pltpu.VMEM((3 * LEAVES, BS), f32),
                pltpu.VMEM((FEATS, points), bf),
                pltpu.VMEM((LEAVES, FEATS, BS), f32),
                pltpu.VMEM((FEATS, CAP * BS), f32),
                pltpu.VMEM((CAP * BS, FEATS), bf),
                pltpu.VMEM((rows, CAP * BS), bf),
                pltpu.VMEM((GRP, CAP, points), f32),
                pltpu.VMEM((rows, points), f32),
                pltpu.VMEM((GRP, 32, 128), bf),
                pltpu.VMEM((GRP, 32, 128), bf),
                pltpu.VMEM((X * Z * C, 32, 128), bf),
                dma((2, 7)),
                dma((2, 7)),
                dma((2, 4)),
                dma((2, 4)),
                dma((GRP,)),
                dma((GRP,)),
                dma((GRP,)),
                dma((GRP,)),
                dma((Z,)),
                dma((Z,)),
                dma((X,)),
                dma((X,)),
                dma,
                dma,
            ],
            compiler_params=pltpu.CompilerParams(
                collective_id=0, has_side_effects=True, vmem_limit_bytes=40 << 20
            ),
        )(
            wanted[0, 0],
            far_source,
            charges,
            positions,
            bases,
            transfers,
            couplings[0],
            near_target[0],
            near_slot[0],
        )

    in_specs = (
        P(None, ("leaf", "grp")),
        P(None, ("leaf", "grp")),
        P(None, ("leaf", "grp")),
        P(("leaf", "grp"), None, None),
        P("leaf", "grp", None),
        P("leaf", None),
        P("leaf", "grp", None, None),
        P("leaf", "grp", None),
        P("leaf", "grp", None),
    )
    out_specs = P(None, ("leaf", "grp"))
    return jax.shard_map(shards, mesh=mesh, in_specs=in_specs, out_specs=out_specs, check_vma=False)
```

time: 455 us -> 69.3 us (0.15)
  the two profiles are of different devices: /device:TPU:1 before, /device:TPU:8 now
where the time goes in v1:
time: 69.3 us; the launch traced here: 69 us
  Pallas kernels  63.8 us (92%)
  local copies, waits for them, and re-layouts  5.18 us (7%)
    pallas_call x1, Pallas kernels, shards(): pl.pallas_call(functools.partial(kernel, dims), out_shape=jax.ShapeDtypeS...  63.8 us
    unnamed x18, local copies, waits for them, and re-layouts  5.18 us

profile of v1, /device:TPU:8, one launch (start us, length us, event | category | flops | bytes accessed | tf_op | source)
XLA Modules:
  0.0 69.0 jit_solution(2180323331460648773)
XLA Ops:
  0.0 0.0 copy-start.3
  0.0 0.0 copy-start.4
  0.0 0.0 copy-start.5
  0.0 0.0 copy-start.6
  0.0 1.0 %copy.10 = bf16[1,512,64]{2,1,0:T(8,128)(2,1)S(1)} copy(bf16[1,512,64]{1,2,0:T(8,128)(2,1)} %param.13) | data formatting | bytes 131072 | tf_op args[4]
  1.0 0.0 copy-start.7
  1.0 0.0 copy-done.3
  1.0 0.0 copy-done.4
  1.1 0.0 copy-done.5
  1.1 0.0 copy-done.6
  1.1 0.6 copy-done.7
  1.7 0.0 copy-start
  1.7 0.9 %copy-done = bf16[64,2048]{1,0:T(8,128)(2,1)S(1)} copy-done((bf16[64,2048]{1,0:T(8,128)(2,1)S(1)}, bf16[64,2048]{1,0:T(8,128)(2,1)}, u32[]{:S(2)}) %copy-start) | copy-done | bytes 262168
  2.6 0.0 copy-start.1
  2.6 0.9 %copy-done.1 = bf16[64,2048]{1,0:T(8,128)(2,1)S(1)} copy-done((bf16[64,2048]{1,0:T(8,128)(2,1)S(1)}, bf16[64,2048]{1,0:T(8,128)(2,1)}, u32[]{:S(2)}) %copy-start.1) | copy-done | bytes 262168
  3.6 0.0 copy-start.2
  3.6 0.9 %copy-done.2 = bf16[16,64,64]{2,1,0:T(8,128)(2,1)S(1)} copy-done((bf16[16,64,64]{2,1,0:T(8,128)(2,1)S(1)}, bf16[16,64,64]{2,1,0:T(8,128)(2,1)}, u32[]{:S(2)}) %copy-start.2) | copy-done | bytes 131096
  4.5 63.8 %shard_map.91 = bf16[64,2048]{1,0:T(8,128)(2,1)S(1)} custom-call(s32[8,8]{1,0:T(8,128)S(1)} %bitcast.5, s32[1,64]{1,0:T(1,128)S(1)} %copy-done.7, bf16[64,2048]{1,0:T(8,128)(2,1)S(1)} %copy-done, bf16[3,2048]{1,0:T(4,128)(2,1)S(1)} %copy-done.3, bf16[64,2048]{1,0:T(8,128)(2,1)S(1)} %copy-done.1, bf16[16,64,64]{2,1,0:T(8,128)(2,1)S(1)} %copy-done.2, ...), custom_call_target="tpu_custom_call" | custom-call | tf_op jit(solution)/shard_map/pallas_call | solution.py:412
  68.3 0.7 %copy.12 = bf16[64,2048]{1,0:T(8,128)(2,1)} copy(bf16[64,2048]{1,0:T(8,128)(2,1)S(1)} %shard_map.91) | data formatting | bytes 524288
Async XLA Ops:
  0.0 1.0 %copy-start.3 = (bf16[3,2048]{1,0:T(4,128)(2,1)S(1)}, bf16[3,2048]{1,0:T(4,128)(2,1)}, u32[]{:S(2)}) copy-start(bf16[3,2048]{1,0:T(4,128)(2,1)} %positions.1) | copy-start | bytes 36868
  0.0 1.0 %copy-start.4 = (s32[1,1,8,8]{3,2,1,0:T(8,128)S(1)}, s32[1,1,8,8]{3,2,1,0:T(8,128)}, u32[]{:S(2)}) copy-start(s32[1,1,8,8]{3,2,1,0:T(8,128)} %param.15) | copy-start | bytes 772
  0.0 1.1 %copy-start.5 = (s32[1,1,512]{2,1,0:T(1,128)S(1)}, s32[1,1,512]{2,1,0:T(1,128)}, u32[]{:S(2)}) copy-start(s32[1,1,512]{2,1,0:T(1,128)} %param.16) | copy-start | bytes 6148
  0.0 1.1 %copy-start.6 = (s32[1,1,512]{2,1,0:T(1,128)S(1)}, s32[1,1,512]{2,1,0:T(1,128)}, u32[]{:S(2)}) copy-start(s32[1,1,512]{2,1,0:T(1,128)} %param.17) | copy-start | bytes 6148
  1.0 0.7 copy-start.7
  1.7 0.9 %copy-start = (bf16[64,2048]{1,0:T(8,128)(2,1)S(1)}, bf16[64,2048]{1,0:T(8,128)(2,1)}, u32[]{:S(2)}) copy-start(bf16[64,2048]{1,0:T(8,128)(2,1)} %charges.1) | copy-start | bytes 786436
  2.6 0.9 %copy-start.1 = (bf16[64,2048]{1,0:T(8,128)(2,1)S(1)}, bf16[64,2048]{1,0:T(8,128)(2,1)}, u32[]{:S(2)}) copy-start(bf16[64,2048]{1,0:T(8,128)(2,1)} %bases.1) | copy-start | bytes 786436
  3.6 0.9 %copy-start.2 = (bf16[16,64,64]{2,1,0:T(8,128)(2,1)S(1)}, bf16[16,64,64]{2,1,0:T(8,128)(2,1)}, u32[]{:S(2)}) copy-start(bf16[16,64,64]{2,1,0:T(8,128)(2,1)} %transfers.1) | copy-start | bytes 393220

commit v2 on v1

--- a/solution.py
+++ b/solution.py
@@ -46,6 +46,16 @@
 
 def kernel(
     dims,
+    wanted_in,
+    far_source_in,
+    charges_in,
+    positions_in,
+    bases_in,
+    transfers_in,
+    couplings_in,
+    near_target_in,
+    near_slot_in,
+    out,
     wanted,
     far_source,
     charges,
@@ -55,7 +65,7 @@
     couplings,
     near_target,
     near_slot,
-    out,
+    in_sem,
     ch0,
     ch1,
     ch2,
@@ -97,6 +107,7 @@
     x_recv,
     core_send,
     core_recv,
+    ready,
 ):
     X, Z, C = dims
     leaf = lax.axis_index("leaf")
@@ -118,6 +129,24 @@
 
     core_peer = ((x * Z + z) * C + (1 - core), y)
 
+    ins = [
+        (charges_in, charges),
+        (positions_in, positions),
+        (bases_in, bases),
+        (transfers_in, transfers),
+        (near_target_in, near_target),
+        (near_slot_in, near_slot),
+        (wanted_in, wanted),
+        (far_source_in, far_source),
+        (couplings_in, couplings),
+    ]
+
+    def fetch(i):
+        return pltpu.make_async_copy(ins[i][0], ins[i][1], in_sem.at[i])
+
+    for i in range(len(ins)):
+        fetch(i).start()
+
     barrier = pltpu.get_barrier_semaphore()
 
     def greet(peer):
@@ -125,12 +154,18 @@
 
     for k in range(1, GRP):
         greet(y_peer(k))
-    for k in range(1, Z):
-        greet(z_peer(k))
     for k in range(1, X):
         greet(x_peer(k))
     if C > 1:
         greet(core_peer)
+    for k in range(1, Z):
+
+        @pl.when(z + k < Z)
+        def _():
+            greet(z_peer(k))
+
+    for i in range(4):
+        fetch(i).wait()
 
     pos = positions[...].astype(f32)
     for d in range(3):
@@ -149,7 +184,13 @@
         partial = term if partial is None else partial + term
     part_up[0] = pack(partial).astype(bf)
 
-    pl.semaphore_wait(barrier, (GRP - 1) + (Z - 1) + (X - 1) + (C - 1))
+    pl.semaphore_wait(barrier, (GRP - 1) + (X - 1) + (C - 1) + z)
+    for k in range(1, Z):
+
+        @pl.when(k <= z)
+        def _():
+            pl.semaphore_signal(ready, inc=1, device_id=z_peer(Z - k), device_id_type=MESH)
+
 
     def exchange(buf, send, recv, k):
         return pltpu.make_async_remote_copy(
@@ -192,16 +233,23 @@
     def slot_of(x_at, z_at):
         return (core * X + x_at) * Z + z_at
 
-    def z_copy(k, z_at):
+    def z_copy(up, k, z_at):
         here = coeffs.at[slot_of(x, z_at)]
         return pltpu.make_async_remote_copy(
             src_ref=here,
             dst_ref=here,
-            send_sem=z_send.at[k],
-            recv_sem=z_recv.at[k],
-            device_id=z_peer(k),
+            send_sem=z_send.at[up, k],
+            recv_sem=z_recv.at[up, k],
+            device_id=z_peer(k if up else Z - k),
             device_id_type=MESH,
         )
+
+    def each_z(up, do):
+        for k in range(1, Z):
+
+            @pl.when(z + k < Z if up else k <= z)
+            def _():
+                do(k)
 
     def x_copy(k, x_at):
         here = coeffs.at[pl.ds(slot_of(x_at, 0), Z)]
@@ -246,6 +294,9 @@
     source_feat[...] = jnp.zeros_like(source_feat)
     for f in (3, 4, 5):
         source_feat[:, f, :] = jnp.ones((LEAVES, BS), f32)
+
+    for i in range(4, 8):
+        fetch(i).wait()
 
     blocks = near_slot.shape[1]
     slot_hot = (
@@ -263,7 +314,7 @@
     for h in range(GRP):
         weight[h] = spread_counts[h * CAP : (h + 1) * CAP, :]
 
-    def near(rel, first=False, last=False):
+    def near(rel, first=False):
         h = (y + (GRP - rel)) % GRP
         rows = place[rel][...].astype(f32)
         px, py, pz = rows[0:16], rows[16:32], rows[32:48]
@@ -297,10 +348,7 @@
                 total = term if total is None else total + term
             if not first:
                 total = total + acc[:, cols]
-            if last:
-                out[:, cols] = total.astype(bf)
-            else:
-                acc[:, cols] = total
+            acc[:, cols] = total
             return carry
 
         lax.fori_loop(0, LEAVES * BS // width, block, 0)
@@ -328,41 +376,53 @@
     for k in range(1, GRP):
         total = total + part_up[k].astype(f32)
     coeffs[slot_of(x, z)] = total.astype(bf)
-    for k in range(1, Z):
-        z_copy(k, z).start()
+    each_z(0, lambda k: z_copy(0, k, z).start())
 
     arrived(0, 1)
     near(1)
-    for k in range(1, Z):
-        z_copy(k, (z + (Z - k)) % Z).wait_recv()
+    arrived(1, 0)
+    near(7)
+    arrived(1, 1)
+    near(2)
+    arrived(2, 0)
+    near(6)
+    arrived(2, 1)
+
+    @pl.when(z < Z - 1)
+    def _():
+        pl.semaphore_wait(ready, Z - 1 - z)
+
+    each_z(1, lambda k: z_copy(1, k, z).start())
+    each_z(1, lambda k: z_copy(0, k, z + k).wait_recv())
+    each_z(0, lambda k: z_copy(1, k, z - k).wait_recv())
     for k in range(1, X):
         x_copy(k, x).start()
-    arrived(1, 0)
-    near(7)
+    near(3)
     for k in range(1, X):
         x_copy(k, (x + (X - k)) % X).wait_recv()
     if C > 1:
         core_copy(core).start()
-    arrived(1, 1)
-    near(2)
-    arrived(2, 0)
-    near(6)
+    near(5)
     if C > 1:
         core_copy(1 - core).wait_recv()
 
-    partial = None
-    rank = couplings.shape[1]
-    for j in range(couplings.shape[0] // rank):
-        source = far_source[0, y * (couplings.shape[0] // rank) + j]
+    rank = couplings.shape[0]
+    count = couplings.shape[1] // rank
+    fetch(8).wait()
+    sums = [None, None]
+    for j in range(count):
+        source = far_source[0, y * count + j]
         slot = source if C == 1 else (source & 1) * (X * Z) + (source >> 1)
-        term = dot_nt(unpack(coeffs[slot]), couplings[j * rank : (j + 1) * rank, :])
-        partial = term if partial is None else partial + term
-    part_down[0] = pack(partial).astype(bf)
+        pair = couplings[:, j // 2 * 2 * rank : (j // 2 + 1) * 2 * rank]
+        term = dot(unpack(coeffs[slot]), pair)
+        sums[j % 2] = term if sums[j % 2] is None else sums[j % 2] + term
+    part_down[0] = pack(sums[0][:, :rank] + sums[1][:, rank:]).astype(bf)
     for k in range(1, GRP):
         exchange(part_down, down_send, down_recv, k).start()
 
-    arrived(2, 1)
-    near(3)
+    arrived(3, 0, left=False)
+    arrived(3, 1, right=False)
+    near(4)
 
     for k in range(1, GRP):
         exchange(part_down, down_send, down_recv, k).wait_recv()
@@ -373,12 +433,7 @@
     for t in range(LEAVES):
         cols = slice(t * BS, (t + 1) * BS)
         leaf_target = dot(target_coeff, transfers[t]).astype(bf)
-        acc[:, cols] += dot(leaf_target, bases[:, cols])
-
-    near(5)
-    arrived(3, 0, left=False)
-    arrived(3, 1, right=False)
-    near(4, last=True)
+        out[:, cols] = (acc[:, cols] + dot(leaf_target, bases[:, cols])).astype(bf)
 
     for k in range(1, GRP):
         exchange(part_up, up_send, up_recv, k).wait_send()
@@ -391,8 +446,8 @@
     ring_pos(True, 3).wait_send()
     ring(True, 3, 0).wait_send()
     ring(False, 3, 1).wait_send()
-    for k in range(1, Z):
-        z_copy(k, z).wait_send()
+    for up in (0, 1):
+        each_z(up, lambda k: z_copy(up, k, z).wait_send())
     for k in range(1, X):
         x_copy(k, x).wait_send()
     if C > 1:
@@ -406,15 +461,27 @@
 
     def shards(charges, positions, bases, transfers, couplings, far_source, wanted, near_target, near_slot):
         vmem = pl.BlockSpec(memory_space=pltpu.VMEM)
-        smem = pl.BlockSpec(memory_space=pltpu.SMEM)
+        hbm = pl.BlockSpec(memory_space=pltpu.HBM)
         rows, points = charges.shape
         dma = pltpu.SemaphoreType.DMA
         return pl.pallas_call(
             functools.partial(kernel, dims),
             out_shape=jax.ShapeDtypeStruct(charges.shape, bf),
-            in_specs=[smem, smem] + [vmem] * 7,
+            in_specs=[hbm] * 9,
             out_specs=vmem,
-            scratch_shapes=[pltpu.VMEM((LEAVES, rows, BS), bf)] * 8
+            scratch_shapes=[
+                pltpu.SMEM(wanted.shape[2:], jnp.int32),
+                pltpu.SMEM(far_source.shape, jnp.int32),
+                pltpu.VMEM(charges.shape, bf),
+                pltpu.VMEM(positions.shape, bf),
+                pltpu.VMEM(bases.shape, bf),
+                pltpu.VMEM(transfers.shape, bf),
+                pltpu.VMEM(couplings.shape[:0:-1], bf),
+                pltpu.VMEM(near_target.shape[1:], jnp.int32),
+                pltpu.VMEM(near_slot.shape[1:], jnp.int32),
+                dma((9,)),
+            ]
+            + [pltpu.VMEM((LEAVES, rows, BS), bf)] * 8
             + [pltpu.VMEM((3 * LEAVES, BS), bf)] * 8
             + [
                 pltpu.VMEM((3 * LEAVES, BS), f32),
@@ -436,15 +503,16 @@
                 dma((GRP,)),
                 dma((GRP,)),
                 dma((GRP,)),
-                dma((Z,)),
-                dma((Z,)),
+                dma((2, Z)),
+                dma((2, Z)),
                 dma((X,)),
                 dma((X,)),
                 dma,
                 dma,
+                pltpu.SemaphoreType.REGULAR,
             ],
             compiler_params=pltpu.CompilerParams(
-                collective_id=0, has_side_effects=True, vmem_limit_bytes=40 << 20
+                collective_id=0, has_side_effects=True, vmem_limit_bytes=56 << 20
             ),
         )(
             wanted[0, 0],
@@ -453,7 +521,7 @@
             positions,
             bases,
             transfers,
-            couplings[0],
+            jnp.swapaxes(couplings[0], 0, 1),
             near_target[0],
             near_slot[0],
         )

time: 69.3 us -> 55.4 us (0.80)
  the two profiles are of different devices: /device:TPU:8 before, /device:TPU:1 now
where the time goes in v2:
time: 55.4 us; the launch traced here: 54.9 us
  Pallas kernels  53.2 us (96%)
  local copies, waits for them, and re-layouts  1.67 us (3%)
    pallas_call x1, Pallas kernels, shards(): pl.pallas_call(functools.partial(kernel, dims), out_shape=jax.ShapeDtypeS...  53.2 us
    unnamed x1, local copies, waits for them, and re-layouts  1.67 us

profile of v2, /device:TPU:1, one launch (start us, length us, event | category | flops | bytes accessed | tf_op | source)
XLA Modules:
  0.0 54.9 jit_solution(12817983192091641294)
XLA Ops:
  0.0 53.2 %shard_map.91 = bf16[64,2048]{1,0:T(8,128)(2,1)} custom-call(s32[8,8]{1,0:T(8,128)} %bitcast.7, s32[1,64]{1,0:T(1,128)} %far_source_in.1, bf16[64,2048]{1,0:T(8,128)(2,1)} %charges_in.1, bf16[3,2048]{1,0:T(4,128)(2,1)} %positions_in.1, bf16[64,2048]{1,0:T(8,128)(2,1)} %bases_in.1, bf16[16,64,64]{2,1,0:T(8,128)(2,1)} %transfers_in.1, ...), custom_call_target="tpu_custom_call" | custom-call | tf_op jit(solution)/shard_map/pallas_call | solution.py:467
  53.3 1.7 %copy.11 = bf16[64,2048]{1,0:T(8,128)(2,1)} copy(bf16[64,2048]{1,0:T(8,128)(2,1)} %shard_map.91) | data formatting | bytes 524288

commit v3 on v2

--- a/solution.py
+++ b/solution.py
@@ -16,6 +16,8 @@
 CAP = 8
 HALF = LEAVES // 2
 FEATS = 16
+QUARTERS = 4
+ROWS = 16
 SOFTEN2 = 0.05 * 0.05
 SCALE = float(BS * BS)
 NT = (((1,), (1,)), ((), ()))
@@ -62,7 +64,6 @@
     positions,
     bases,
     transfers,
-    couplings,
     near_target,
     near_slot,
     in_sem,
@@ -90,9 +91,12 @@
     charge_sel,
     weight,
     acc,
+    up_out,
     part_up,
+    sibling,
     part_down,
     coeffs,
+    panels,
     ring_send,
     ring_recv,
     pos_send,
@@ -107,6 +111,8 @@
     x_recv,
     core_send,
     core_recv,
+    panel_send,
+    panel_recv,
     ready,
 ):
     X, Z, C = dims
@@ -115,6 +121,8 @@
     x = leaf // (Z * C)
     z = (leaf // C) % Z
     core = leaf % C
+    quarter = y % QUARTERS
+    first_y = y - quarter
     chunk = [ch0, ch1, ch2, ch3, ch4, ch5, ch6, ch7]
     place = [ps0, ps1, ps2, ps3, ps4, ps5, ps6, ps7]
 
@@ -138,7 +146,7 @@
         (near_slot_in, near_slot),
         (wanted_in, wanted),
         (far_source_in, far_source),
-        (couplings_in, couplings),
+        (couplings_in.at[pl.ds(pl.multiple_of(quarter * ROWS, ROWS), ROWS)], panels.at[0]),
     ]
 
     def fetch(i):
@@ -179,10 +187,12 @@
     partial = None
     for t in range(LEAVES):
         cols = slice(t * BS, (t + 1) * BS)
-        leaf_coeff = dot_nt(charges[:, cols], bases[:, cols]).astype(bf)
-        term = dot_nt(leaf_coeff, transfers[t])
+        leaf_coeff = dot_nt(bases[:, cols], charges[:, cols]).astype(bf)
+        term = dot(transfers[t], leaf_coeff)
         partial = term if partial is None else partial + term
-    part_up[0] = pack(partial).astype(bf)
+    partial = jnp.concatenate([partial, partial], axis=1).astype(bf)
+    for q in range(QUARTERS):
+        up_out[q] = partial[q * ROWS : (q + 1) * ROWS, :]
 
     pl.semaphore_wait(barrier, (GRP - 1) + (X - 1) + (C - 1) + z)
     for k in range(1, Z):
@@ -192,13 +202,34 @@
             pl.semaphore_signal(ready, inc=1, device_id=z_peer(Z - k), device_id_type=MESH)
 
 
-    def exchange(buf, send, recv, k):
-        return pltpu.make_async_remote_copy(
-            src_ref=buf.at[0],
-            dst_ref=buf.at[k],
-            send_sem=send.at[k],
-            recv_sem=recv.at[k],
+    def up_copy(k):
+        return pltpu.make_async_remote_copy(
+            src_ref=up_out.at[(y + k) % QUARTERS],
+            dst_ref=part_up.at[k],
+            send_sem=up_send.at[k],
+            recv_sem=up_recv.at[k],
             device_id=y_peer(k),
+            device_id_type=MESH,
+        )
+
+    def down_copy(k):
+        return pltpu.make_async_remote_copy(
+            src_ref=part_down.at[0],
+            dst_ref=part_down.at[k],
+            send_sem=down_send.at[k],
+            recv_sem=down_recv.at[k],
+            device_id=y_peer(k),
+            device_id_type=MESH,
+        )
+
+    def panel_copy(k):
+        to = (quarter + k) % QUARTERS
+        return pltpu.make_async_remote_copy(
+            src_ref=couplings_in.at[pl.ds(pl.multiple_of(to * ROWS, ROWS), ROWS)],
+            dst_ref=panels.at[k],
+            send_sem=panel_send.at[k],
+            recv_sem=panel_recv.at[k],
+            device_id=(leaf, first_y + to),
             device_id_type=MESH,
         )
 
@@ -231,7 +262,7 @@
         )
 
     def slot_of(x_at, z_at):
-        return (core * X + x_at) * Z + z_at
+        return x_at * Z + z_at
 
     def z_copy(up, k, z_at):
         here = coeffs.at[slot_of(x, z_at)]
@@ -262,11 +293,10 @@
             device_id_type=MESH,
         )
 
-    def core_copy(core_at):
-        here = coeffs.at[pl.ds(core_at * (X * Z), X * Z)]
-        return pltpu.make_async_remote_copy(
-            src_ref=here,
-            dst_ref=here,
+    def core_copy():
+        return pltpu.make_async_remote_copy(
+            src_ref=sibling.at[0],
+            dst_ref=sibling.at[1],
             send_sem=core_send,
             recv_sem=core_recv,
             device_id=core_peer,
@@ -274,7 +304,7 @@
         )
 
     for k in range(1, GRP):
-        exchange(part_up, up_send, up_recv, k).start()
+        up_copy(k).start()
     for right in (True, False):
         ring_pos(right, 0).start()
     for half in (0, 1):
@@ -368,64 +398,80 @@
                     ring(way, 3, half).start()
 
     near(0, first=True)
+
+    for k in range(1, GRP):
+        up_copy(k).wait_recv()
+    total = up_out[quarter].astype(f32)
+    for k in range(1, GRP):
+        total = total + part_up[k].astype(f32)
+    if C > 1:
+        sibling[0] = total.astype(bf)
+        core_copy().start()
     arrived(0, 0)
-
-    for k in range(1, GRP):
-        exchange(part_up, up_send, up_recv, k).wait_recv()
-    total = part_up[0].astype(f32)
-    for k in range(1, GRP):
-        total = total + part_up[k].astype(f32)
+    if C > 1:
+        core_copy().wait_recv()
+        side = lax.broadcasted_iota(jnp.int32, total.shape, 1) // (total.shape[1] // 2)
+        total = jnp.where(side == core, total.astype(bf).astype(f32), sibling[1].astype(f32))
     coeffs[slot_of(x, z)] = total.astype(bf)
     each_z(0, lambda k: z_copy(0, k, z).start())
 
     arrived(0, 1)
+    for k in range(1, QUARTERS):
+        panel_copy(k).start()
     near(1)
     arrived(1, 0)
     near(7)
     arrived(1, 1)
     near(2)
     arrived(2, 0)
-    near(6)
-    arrived(2, 1)
 
     @pl.when(z < Z - 1)
     def _():
         pl.semaphore_wait(ready, Z - 1 - z)
 
     each_z(1, lambda k: z_copy(1, k, z).start())
+    near(6)
+    arrived(2, 1)
     each_z(1, lambda k: z_copy(0, k, z + k).wait_recv())
     each_z(0, lambda k: z_copy(1, k, z - k).wait_recv())
     for k in range(1, X):
         x_copy(k, x).start()
     near(3)
+    near(5)
+
     for k in range(1, X):
         x_copy(k, (x + (X - k)) % X).wait_recv()
-    if C > 1:
-        core_copy(core).start()
-    near(5)
-    if C > 1:
-        core_copy(1 - core).wait_recv()
-
-    rank = couplings.shape[0]
-    count = couplings.shape[1] // rank
     fetch(8).wait()
-    sums = [None, None]
-    for j in range(count):
-        source = far_source[0, y * count + j]
-        slot = source if C == 1 else (source & 1) * (X * Z) + (source >> 1)
-        pair = couplings[:, j // 2 * 2 * rank : (j // 2 + 1) * 2 * rank]
-        term = dot(unpack(coeffs[slot]), pair)
-        sums[j % 2] = term if sums[j % 2] is None else sums[j % 2] + term
-    part_down[0] = pack(sums[0][:, :rank] + sums[1][:, rank:]).astype(bf)
-    for k in range(1, GRP):
-        exchange(part_down, down_send, down_recv, k).start()
+    for k in range(1, QUARTERS):
+        panel_copy(k).wait_recv()
+    rank = couplings_in.shape[0]
+    count = couplings_in.shape[1] // rank
+    terms = []
+    for odd in (0, 1):
+        coeff_rows, panel_rows = [], []
+        for k in range(QUARTERS):
+            owner = first_y + (quarter + (QUARTERS - k)) % QUARTERS
+            for j in range(odd, count, 2):
+                source = far_source[0, owner * count + j]
+                if C == 1:
+                    rows = coeffs[source].astype(f32)[:, :rank]
+                else:
+                    both = coeffs[source >> 1].astype(f32)
+                    rows = jnp.where((source & 1) == 0, both[:, :rank], both[:, rank:])
+                coeff_rows.append(rows)
+                panel_rows.append(panels[k, :, (j - odd) * rank : (j - odd + 2) * rank])
+        left = jnp.concatenate(coeff_rows, axis=0).T.astype(bf)
+        terms.append(dot(left, jnp.concatenate(panel_rows, axis=0)))
+    part_down[0] = pack(terms[0][:, :rank] + terms[1][:, rank:]).astype(bf)
+    for k in range(1, GRP):
+        down_copy(k).start()
 
     arrived(3, 0, left=False)
     arrived(3, 1, right=False)
     near(4)
 
     for k in range(1, GRP):
-        exchange(part_down, down_send, down_recv, k).wait_recv()
+        down_copy(k).wait_recv()
     total = part_down[0].astype(f32)
     for k in range(1, GRP):
         total = total + part_down[k].astype(f32)
@@ -436,8 +482,8 @@
         out[:, cols] = (acc[:, cols] + dot(leaf_target, bases[:, cols])).astype(bf)
 
     for k in range(1, GRP):
-        exchange(part_up, up_send, up_recv, k).wait_send()
-        exchange(part_down, down_send, down_recv, k).wait_send()
+        up_copy(k).wait_send()
+        down_copy(k).wait_send()
     for right in (True, False):
         for step in range(3):
             ring_pos(right, step).wait_send()
@@ -450,8 +496,10 @@
         each_z(up, lambda k: z_copy(up, k, z).wait_send())
     for k in range(1, X):
         x_copy(k, x).wait_send()
+    for k in range(1, QUARTERS):
+        panel_copy(k).wait_send()
     if C > 1:
-        core_copy(core).wait_send()
+        core_copy().wait_send()
 
 
 def solution(mesh):
@@ -476,7 +524,6 @@
                 pltpu.VMEM(positions.shape, bf),
                 pltpu.VMEM(bases.shape, bf),
                 pltpu.VMEM(transfers.shape, bf),
-                pltpu.VMEM(couplings.shape[:0:-1], bf),
                 pltpu.VMEM(near_target.shape[1:], jnp.int32),
                 pltpu.VMEM(near_slot.shape[1:], jnp.int32),
                 dma((9,)),
@@ -492,9 +539,12 @@
                 pltpu.VMEM((rows, CAP * BS), bf),
                 pltpu.VMEM((GRP, CAP, points), f32),
                 pltpu.VMEM((rows, points), f32),
+                pltpu.VMEM((QUARTERS, ROWS, 128), bf),
+                pltpu.VMEM((GRP, ROWS, 128), bf),
+                pltpu.VMEM((2, ROWS, 128), bf),
                 pltpu.VMEM((GRP, 32, 128), bf),
-                pltpu.VMEM((GRP, 32, 128), bf),
-                pltpu.VMEM((X * Z * C, 32, 128), bf),
+                pltpu.VMEM((X * Z, ROWS, 128), bf),
+                pltpu.VMEM((QUARTERS, ROWS, couplings.shape[1]), bf),
                 dma((2, 7)),
                 dma((2, 7)),
                 dma((2, 4)),
@@ -509,6 +559,8 @@
                 dma((X,)),
                 dma,
                 dma,
+                dma((QUARTERS,)),
+                dma((QUARTERS,)),
                 pltpu.SemaphoreType.REGULAR,
             ],
             compiler_params=pltpu.CompilerParams(

time: 55.4 us -> 51.8 us (0.935)
  the two profiles are of different devices: /device:TPU:1 before, /device:TPU:8 now
where the time goes in v3:
time: 51.8 us; the launch traced here: 51.6 us
  Pallas kernels  49.9 us (96%)
  local copies, waits for them, and re-layouts  1.67 us (3%)
    pallas_call x1, Pallas kernels, shards(): pl.pallas_call(functools.partial(kernel, dims), out_shape=jax.ShapeDtypeS...  49.9 us
    unnamed x1, local copies, waits for them, and re-layouts  1.67 us

profile of v3, /device:TPU:8, one launch (start us, length us, event | category | flops | bytes accessed | tf_op | source)
XLA Modules:
  0.0 51.6 jit_solution(9055421269772455252)
XLA Ops:
  0.0 49.9 %shard_map.91 = bf16[64,2048]{1,0:T(8,128)(2,1)} custom-call(s32[8,8]{1,0:T(8,128)} %bitcast.7, s32[1,64]{1,0:T(1,128)} %far_source_in.1, bf16[64,2048]{1,0:T(8,128)(2,1)} %charges_in.1, bf16[3,2048]{1,0:T(4,128)(2,1)} %positions_in.1, bf16[64,2048]{1,0:T(8,128)(2,1)} %bases_in.1, bf16[16,64,64]{2,1,0:T(8,128)(2,1)} %transfers_in.1, ...), custom_call_target="tpu_custom_call" | custom-call | tf_op jit(solution)/shard_map/pallas_call | solution.py:515
  49.9 1.7 %copy.11 = bf16[64,2048]{1,0:T(8,128)(2,1)} copy(bf16[64,2048]{1,0:T(8,128)(2,1)} %shard_map.91) | data formatting | bytes 524288

commit v4 on v3

--- a/solution.py
+++ b/solution.py
@@ -15,7 +15,8 @@
 BS = 128
 CAP = 8
 HALF = LEAVES // 2
-FEATS = 16
+FEATS = 9
+LANES = 256
 QUARTERS = 4
 ROWS = 16
 SOFTEN2 = 0.05 * 0.05
@@ -85,9 +86,7 @@
     ps7,
     pos_rows,
     target_feat,
-    source_feat,
     feat_sel,
-    feat_sel_t,
     charge_sel,
     weight,
     acc,
@@ -113,7 +112,9 @@
     core_recv,
     panel_send,
     panel_recv,
-    ready,
+    ready_z,
+    ready_x,
+    ready_core,
 ):
     X, Z, C = dims
     leaf = lax.axis_index("leaf")
@@ -160,20 +161,41 @@
     def greet(peer):
         pl.semaphore_signal(barrier, inc=1, device_id=peer, device_id_type=MESH)
 
+    first_column = (x + y + core) == 0
+
+    def order(z_at):
+        return jnp.where(first_column & (z_at == 0), Z - 1, 2 * z_at)
+
+    def z_speaks(k):
+        return order(z) < order((z + k) % Z)
+
+    def answer(semaphore, peer):
+        pl.semaphore_signal(semaphore, inc=1, device_id=peer, device_id_type=MESH)
+
     for k in range(1, GRP):
         greet(y_peer(k))
+    if C > 1:
+
+        @pl.when(core == 1)
+        def _():
+            greet(core_peer)
+
     for k in range(1, X):
-        greet(x_peer(k))
-    if C > 1:
-        greet(core_peer)
+
+        @pl.when(x >= k)
+        def _():
+            greet(x_peer(X - k))
+
     for k in range(1, Z):
 
-        @pl.when(z + k < Z)
+        @pl.when(z_speaks(k))
         def _():
             greet(z_peer(k))
 
-    for i in range(4):
-        fetch(i).wait()
+    heard_z = sum([jnp.where(z_speaks(k), 0, 1) for k in range(1, Z)], 0)
+
+    fetch(0).wait()
+    fetch(1).wait()
 
     pos = positions[...].astype(f32)
     for d in range(3):
@@ -184,6 +206,129 @@
     for t in range(LEAVES):
         ch0[t] = charges[:, t * BS : (t + 1) * BS]
 
+    pl.semaphore_wait(barrier, (GRP - 1) + (X - 1 - x) + (C - 1) * (1 - core) + heard_z)
+
+    def up_copy(k):
+        return pltpu.make_async_remote_copy(
+            src_ref=up_out.at[(y + k) % QUARTERS],
+            dst_ref=part_up.at[k],
+            send_sem=up_send.at[k],
+            recv_sem=up_recv.at[k],
+            device_id=y_peer(k),
+            device_id_type=MESH,
+        )
+
+    def down_copy(k):
+        return pltpu.make_async_remote_copy(
+            src_ref=part_down.at[0],
+            dst_ref=part_down.at[k],
+            send_sem=down_send.at[k],
+            recv_sem=down_recv.at[k],
+            device_id=y_peer(k),
+            device_id_type=MESH,
+        )
+
+    def panel_copy(k):
+        to = (quarter + k) % QUARTERS
+        return pltpu.make_async_remote_copy(
+            src_ref=couplings_in.at[pl.ds(pl.multiple_of(to * ROWS, ROWS), ROWS)],
+            dst_ref=panels.at[k],
+            send_sem=panel_send.at[k],
+            recv_sem=panel_recv.at[k],
+            device_id=(leaf, first_y + to),
+            device_id_type=MESH,
+        )
+
+    def ring(right, step, half):
+        src = step if right else (GRP - step) % GRP
+        dst = step + 1 if right else GRP - step - 1
+        part = pl.ds(half * HALF, HALF)
+        way = 0 if right else 1
+        slot = 2 * step + (half if step < 3 else 0)
+        return pltpu.make_async_remote_copy(
+            src_ref=chunk[src].at[part],
+            dst_ref=chunk[dst].at[part],
+            send_sem=ring_send.at[way, slot],
+            recv_sem=ring_recv.at[way, slot],
+            device_id=y_peer(1 if right else GRP - 1),
+            device_id_type=MESH,
+        )
+
+    def ring_pos(right, step):
+        src = step if right else (GRP - step) % GRP
+        dst = step + 1 if right else GRP - step - 1
+        way = 0 if right else 1
+        return pltpu.make_async_remote_copy(
+            src_ref=place[src],
+            dst_ref=place[dst],
+            send_sem=pos_send.at[way, step],
+            recv_sem=pos_recv.at[way, step],
+            device_id=y_peer(1 if right else GRP - 1),
+            device_id_type=MESH,
+        )
+
+    def slot_of(x_at, z_at):
+        return x_at * Z + z_at
+
+    def z_copy(k, z_at):
+        here = coeffs.at[slot_of(x, z_at)]
+        return pltpu.make_async_remote_copy(
+            src_ref=here,
+            dst_ref=here,
+            send_sem=z_send.at[k],
+            recv_sem=z_recv.at[k],
+            device_id=z_peer(k),
+            device_id_type=MESH,
+        )
+
+    def each_z(speaks, do):
+        for k in range(1, Z):
+
+            @pl.when(z_speaks(k) if speaks else jnp.logical_not(z_speaks(k)))
+            def _():
+                do(k)
+
+    def x_copy(k, x_at):
+        here = coeffs.at[pl.ds(slot_of(x_at, 0), Z)]
+        return pltpu.make_async_remote_copy(
+            src_ref=here,
+            dst_ref=here,
+            send_sem=x_send.at[k],
+            recv_sem=x_recv.at[k],
+            device_id=x_peer(k),
+            device_id_type=MESH,
+        )
+
+    def core_copy():
+        return pltpu.make_async_remote_copy(
+            src_ref=sibling.at[0],
+            dst_ref=sibling.at[1],
+            send_sem=core_send,
+            recv_sem=core_recv,
+            device_id=core_peer,
+            device_id_type=MESH,
+        )
+
+    for right in (True, False):
+        ring_pos(right, 0).start()
+        ring(right, 0, 0).start()
+
+    if C > 1:
+
+        @pl.when(core == 0)
+        def _():
+            answer(ready_core, core_peer)
+
+    for k in range(1, X):
+
+        @pl.when(x + k < X)
+        def _():
+            answer(ready_x, x_peer(k))
+
+    each_z(False, lambda k: answer(ready_z, z_peer(k)))
+
+    fetch(2).wait()
+    fetch(3).wait()
     partial = None
     for t in range(LEAVES):
         cols = slice(t * BS, (t + 1) * BS)
@@ -193,137 +338,18 @@
     partial = jnp.concatenate([partial, partial], axis=1).astype(bf)
     for q in range(QUARTERS):
         up_out[q] = partial[q * ROWS : (q + 1) * ROWS, :]
-
-    pl.semaphore_wait(barrier, (GRP - 1) + (X - 1) + (C - 1) + z)
-    for k in range(1, Z):
-
-        @pl.when(k <= z)
-        def _():
-            pl.semaphore_signal(ready, inc=1, device_id=z_peer(Z - k), device_id_type=MESH)
-
-
-    def up_copy(k):
-        return pltpu.make_async_remote_copy(
-            src_ref=up_out.at[(y + k) % QUARTERS],
-            dst_ref=part_up.at[k],
-            send_sem=up_send.at[k],
-            recv_sem=up_recv.at[k],
-            device_id=y_peer(k),
-            device_id_type=MESH,
-        )
-
-    def down_copy(k):
-        return pltpu.make_async_remote_copy(
-            src_ref=part_down.at[0],
-            dst_ref=part_down.at[k],
-            send_sem=down_send.at[k],
-            recv_sem=down_recv.at[k],
-            device_id=y_peer(k),
-            device_id_type=MESH,
-        )
-
-    def panel_copy(k):
-        to = (quarter + k) % QUARTERS
-        return pltpu.make_async_remote_copy(
-            src_ref=couplings_in.at[pl.ds(pl.multiple_of(to * ROWS, ROWS), ROWS)],
-            dst_ref=panels.at[k],
-            send_sem=panel_send.at[k],
-            recv_sem=panel_recv.at[k],
-            device_id=(leaf, first_y + to),
-            device_id_type=MESH,
-        )
-
-    def ring(right, step, half):
-        src = step if right else (GRP - step) % GRP
-        dst = step + 1 if right else GRP - step - 1
-        part = pl.ds(half * HALF, HALF)
-        way = 0 if right else 1
-        slot = 2 * step + (half if step < 3 else 0)
-        return pltpu.make_async_remote_copy(
-            src_ref=chunk[src].at[part],
-            dst_ref=chunk[dst].at[part],
-            send_sem=ring_send.at[way, slot],
-            recv_sem=ring_recv.at[way, slot],
-            device_id=y_peer(1 if right else GRP - 1),
-            device_id_type=MESH,
-        )
-
-    def ring_pos(right, step):
-        src = step if right else (GRP - step) % GRP
-        dst = step + 1 if right else GRP - step - 1
-        way = 0 if right else 1
-        return pltpu.make_async_remote_copy(
-            src_ref=place[src],
-            dst_ref=place[dst],
-            send_sem=pos_send.at[way, step],
-            recv_sem=pos_recv.at[way, step],
-            device_id=y_peer(1 if right else GRP - 1),
-            device_id_type=MESH,
-        )
-
-    def slot_of(x_at, z_at):
-        return x_at * Z + z_at
-
-    def z_copy(up, k, z_at):
-        here = coeffs.at[slot_of(x, z_at)]
-        return pltpu.make_async_remote_copy(
-            src_ref=here,
-            dst_ref=here,
-            send_sem=z_send.at[up, k],
-            recv_sem=z_recv.at[up, k],
-            device_id=z_peer(k if up else Z - k),
-            device_id_type=MESH,
-        )
-
-    def each_z(up, do):
-        for k in range(1, Z):
-
-            @pl.when(z + k < Z if up else k <= z)
-            def _():
-                do(k)
-
-    def x_copy(k, x_at):
-        here = coeffs.at[pl.ds(slot_of(x_at, 0), Z)]
-        return pltpu.make_async_remote_copy(
-            src_ref=here,
-            dst_ref=here,
-            send_sem=x_send.at[k],
-            recv_sem=x_recv.at[k],
-            device_id=x_peer(k),
-            device_id_type=MESH,
-        )
-
-    def core_copy():
-        return pltpu.make_async_remote_copy(
-            src_ref=sibling.at[0],
-            dst_ref=sibling.at[1],
-            send_sem=core_send,
-            recv_sem=core_recv,
-            device_id=core_peer,
-            device_id_type=MESH,
-        )
-
     for k in range(1, GRP):
         up_copy(k).start()
     for right in (True, False):
-        ring_pos(right, 0).start()
-    for half in (0, 1):
-        for right in (True, False):
-            ring(right, 0, half).start()
+        ring(right, 0, 1).start()
 
     norm = jnp.sum(pos * pos, axis=0, keepdims=True) + SOFTEN2
     high, middle, low = pieces(norm)
     one = jnp.ones_like(norm)
-    target_feat[...] = (
-        jnp.concatenate(
-            [-2.0 * pos, high, middle, low, one, one, one, jnp.zeros((FEATS - 9, norm.shape[1]), f32)],
-            axis=0,
-        )
-        * SCALE
-    ).astype(bf)
-    source_feat[...] = jnp.zeros_like(source_feat)
-    for f in (3, 4, 5):
-        source_feat[:, f, :] = jnp.ones((LEAVES, BS), f32)
+    target_feat[...] = jnp.zeros_like(target_feat)
+    for f, v in enumerate((-2.0 * pos[0:1], -2.0 * pos[1:2], -2.0 * pos[2:3], high, middle, low, one, one, one)):
+        rows = jnp.broadcast_to(v * SCALE, (LEAVES, v.shape[1]))
+        target_feat[f * LEAVES : (f + 1) * LEAVES, :] = rows.astype(bf)
 
     for i in range(4, 8):
         fetch(i).wait()
@@ -344,44 +370,39 @@
     for h in range(GRP):
         weight[h] = spread_counts[h * CAP : (h + 1) * CAP, :]
 
-    def near(rel, first=False):
+    def near(rel, first=False, last=False):
         h = (y + (GRP - rel)) % GRP
         rows = place[rel][...].astype(f32)
         px, py, pz = rows[0:16], rows[16:32], rows[32:48]
+        ones = jnp.ones_like(px)
         parts = pieces(px * px + py * py + pz * pz)
-        for f, v in zip((0, 1, 2, 6, 7, 8), (px, py, pz) + parts):
-            source_feat[:, f, :] = v
+        pad = jnp.zeros((LANES - FEATS * LEAVES, BS), f32)
+        feats = jnp.concatenate((px, py, pz, ones, ones, ones) + parts + (pad,), axis=0)
+        feats = feats.T
+        lane_leaf = lax.broadcasted_iota(jnp.int32, feats.shape, 1) % LEAVES
         for c in range(CAP):
             at = wanted[h, c]
-            cols = slice(c * BS, (c + 1) * BS)
-            charge_sel[:, cols] = chunk[rel][at]
-            feat_sel[:, cols] = source_feat[at]
-        feat_sel_t[...] = feat_sel[...].T.astype(bf)
-        width, depth = 1024, 512
-
-        def block(i, carry):
-            cols = pl.ds(pl.multiple_of(i * width, width), width)
-            targets = target_feat[:, cols]
-            w = weight[h, :, cols].astype(bf)
-            total = None
-            for k in range(0, CAP * BS, depth):
-                dist = dot(feat_sel_t[k : k + depth, :], targets)
-                g = lax.rsqrt(dist.astype(bf))
-                g = jnp.concatenate(
-                    [
-                        g[j * BS : (j + 1) * BS, :] * w[k // BS + j : k // BS + j + 1, :]
-                        for j in range(depth // BS)
-                    ],
-                    axis=0,
-                )
-                term = dot(charge_sel[:, k : k + depth], g)
-                total = term if total is None else total + term
-            if not first:
-                total = total + acc[:, cols]
-            acc[:, cols] = total
-            return carry
-
-        lax.fori_loop(0, LEAVES * BS // width, block, 0)
+            charge_sel[:, c * BS : (c + 1) * BS] = chunk[rel][at]
+            feat_sel[c * BS : (c + 1) * BS, :] = jnp.where(lane_leaf == at, feats, 0.0).astype(bf)
+        depth = 256
+        total = None if first else acc[...]
+        w = weight[h].astype(bf)
+        for k in range(0, CAP * BS, depth):
+            dist = dot(feat_sel[k : k + depth, :], target_feat[...])
+            g = lax.rsqrt(dist.astype(bf))
+            g = jnp.concatenate(
+                [
+                    g[j * BS : (j + 1) * BS, :] * w[k // BS + j : k // BS + j + 1, :]
+                    for j in range(depth // BS)
+                ],
+                axis=0,
+            )
+            term = dot(charge_sel[:, k : k + depth], g)
+            total = term if total is None else total + term
+        if last:
+            out[...] = total.astype(bf)
+        else:
+            acc[...] = total
 
     def arrived(step, half, right=True, left=True):
         for way in (True, False):
@@ -397,8 +418,6 @@
                 elif step == 2 and (half == 0) == way:
                     ring(way, 3, half).start()
 
-    near(0, first=True)
-
     for k in range(1, GRP):
         up_copy(k).wait_recv()
     total = up_out[quarter].astype(f32)
@@ -406,6 +425,11 @@
         total = total + part_up[k].astype(f32)
     if C > 1:
         sibling[0] = total.astype(bf)
+
+        @pl.when(core == 1)
+        def _():
+            pl.semaphore_wait(ready_core, 1)
+
         core_copy().start()
     arrived(0, 0)
     if C > 1:
@@ -413,8 +437,9 @@
         side = lax.broadcasted_iota(jnp.int32, total.shape, 1) // (total.shape[1] // 2)
         total = jnp.where(side == core, total.astype(bf).astype(f32), sibling[1].astype(f32))
     coeffs[slot_of(x, z)] = total.astype(bf)
-    each_z(0, lambda k: z_copy(0, k, z).start())
-
+    each_z(False, lambda k: z_copy(k, z).start())
+
+    near(0, first=True)
     arrived(0, 1)
     for k in range(1, QUARTERS):
         panel_copy(k).start()
@@ -422,22 +447,24 @@
     arrived(1, 0)
     near(7)
     arrived(1, 1)
+
+    @pl.when(heard_z < Z - 1)
+    def _():
+        pl.semaphore_wait(ready_z, Z - 1 - heard_z)
+
+    each_z(True, lambda k: z_copy(k, z).start())
     near(2)
-    arrived(2, 0)
-
-    @pl.when(z < Z - 1)
+    for k in range(1, Z):
+        z_copy(k, (z + (Z - k)) % Z).wait_recv()
+
+    @pl.when(x > 0)
     def _():
-        pl.semaphore_wait(ready, Z - 1 - z)
-
-    each_z(1, lambda k: z_copy(1, k, z).start())
-    near(6)
-    arrived(2, 1)
-    each_z(1, lambda k: z_copy(0, k, z + k).wait_recv())
-    each_z(0, lambda k: z_copy(1, k, z - k).wait_recv())
+        pl.semaphore_wait(ready_x, x)
+
     for k in range(1, X):
         x_copy(k, x).start()
-    near(3)
-    near(5)
+    arrived(2, 0)
+    near(6)
 
     for k in range(1, X):
         x_copy(k, (x + (X - k)) % X).wait_recv()
@@ -466,9 +493,9 @@
     for k in range(1, GRP):
         down_copy(k).start()
 
-    arrived(3, 0, left=False)
-    arrived(3, 1, right=False)
-    near(4)
+    arrived(2, 1)
+    near(3)
+    near(5)
 
     for k in range(1, GRP):
         down_copy(k).wait_recv()
@@ -479,7 +506,11 @@
     for t in range(LEAVES):
         cols = slice(t * BS, (t + 1) * BS)
         leaf_target = dot(target_coeff, transfers[t]).astype(bf)
-        out[:, cols] = (acc[:, cols] + dot(leaf_target, bases[:, cols])).astype(bf)
+        acc[:, cols] += dot(leaf_target, bases[:, cols])
+
+    arrived(3, 0, left=False)
+    arrived(3, 1, right=False)
+    near(4, last=True)
 
     for k in range(1, GRP):
         up_copy(k).wait_send()
@@ -492,8 +523,8 @@
     ring_pos(True, 3).wait_send()
     ring(True, 3, 0).wait_send()
     ring(False, 3, 1).wait_send()
-    for up in (0, 1):
-        each_z(up, lambda k: z_copy(up, k, z).wait_send())
+    for k in range(1, Z):
+        z_copy(k, z).wait_send()
     for k in range(1, X):
         x_copy(k, x).wait_send()
     for k in range(1, QUARTERS):
@@ -532,10 +563,8 @@
             + [pltpu.VMEM((3 * LEAVES, BS), bf)] * 8
             + [
                 pltpu.VMEM((3 * LEAVES, BS), f32),
-                pltpu.VMEM((FEATS, points), bf),
-                pltpu.VMEM((LEAVES, FEATS, BS), f32),
-                pltpu.VMEM((FEATS, CAP * BS), f32),
-                pltpu.VMEM((CAP * BS, FEATS), bf),
+                pltpu.VMEM((LANES, points), bf),
+                pltpu.VMEM((CAP * BS, LANES), bf),
                 pltpu.VMEM((rows, CAP * BS), bf),
                 pltpu.VMEM((GRP, CAP, points), f32),
                 pltpu.VMEM((rows, points), f32),
@@ -553,14 +582,16 @@
                 dma((GRP,)),
                 dma((GRP,)),
                 dma((GRP,)),
-                dma((2, Z)),
-                dma((2, Z)),
+                dma((Z,)),
+                dma((Z,)),
                 dma((X,)),
                 dma((X,)),
                 dma,
                 dma,
                 dma((QUARTERS,)),
                 dma((QUARTERS,)),
+                pltpu.SemaphoreType.REGULAR,
+                pltpu.SemaphoreType.REGULAR,
                 pltpu.SemaphoreType.REGULAR,
             ],
             compiler_params=pltpu.CompilerParams(

time: 51.8 us -> 54.5 us (1.052)
  the two profiles are of different devices: /device:TPU:8 before, /device:TPU:1 now
where the time goes in v4:
time: 54.5 us; the launch traced here: 54.4 us
  Pallas kernels  52.7 us (97%)
  local copies, waits for them, and re-layouts  1.67 us (3%)
    pallas_call x1, Pallas kernels, shards(): pl.pallas_call(functools.partial(kernel, dims), out_shape=jax.ShapeDtypeS...  52.7 us
    unnamed x1, local copies, waits for them, and re-layouts  1.67 us

profile of v4, /device:TPU:1, one launch (start us, length us, event | category | flops | bytes accessed | tf_op | source)
XLA Modules:
  0.0 54.4 jit_solution(638627535844117060)
XLA Ops:
  0.0 52.7 %shard_map.91 = bf16[64,2048]{1,0:T(8,128)(2,1)} custom-call(s32[8,8]{1,0:T(8,128)} %bitcast.7, s32[1,64]{1,0:T(1,128)} %far_source_in.1, bf16[64,2048]{1,0:T(8,128)(2,1)} %charges_in.1, bf16[3,2048]{1,0:T(4,128)(2,1)} %positions_in.1, bf16[64,2048]{1,0:T(8,128)(2,1)} %bases_in.1, bf16[16,64,64]{2,1,0:T(8,128)(2,1)} %transfers_in.1, ...), custom_call_target="tpu_custom_call" | custom-call | tf_op jit(solution)/shard_map/pallas_call | solution.py:546
  52.7 1.7 %copy.11 = bf16[64,2048]{1,0:T(8,128)(2,1)} copy(bf16[64,2048]{1,0:T(8,128)(2,1)} %shard_map.91) | data formatting | bytes 524288

commit v5 on v3

--- a/solution.py
+++ b/solution.py
@@ -15,7 +15,8 @@
 BS = 128
 CAP = 8
 HALF = LEAVES // 2
-FEATS = 16
+FEATS = 9
+LANES = 256
 QUARTERS = 4
 ROWS = 16
 SOFTEN2 = 0.05 * 0.05
@@ -85,9 +86,7 @@
     ps7,
     pos_rows,
     target_feat,
-    source_feat,
     feat_sel,
-    feat_sel_t,
     charge_sel,
     weight,
     acc,
@@ -314,16 +313,10 @@
     norm = jnp.sum(pos * pos, axis=0, keepdims=True) + SOFTEN2
     high, middle, low = pieces(norm)
     one = jnp.ones_like(norm)
-    target_feat[...] = (
-        jnp.concatenate(
-            [-2.0 * pos, high, middle, low, one, one, one, jnp.zeros((FEATS - 9, norm.shape[1]), f32)],
-            axis=0,
-        )
-        * SCALE
-    ).astype(bf)
-    source_feat[...] = jnp.zeros_like(source_feat)
-    for f in (3, 4, 5):
-        source_feat[:, f, :] = jnp.ones((LEAVES, BS), f32)
+    target_feat[...] = jnp.zeros_like(target_feat)
+    for f, v in enumerate((-2.0 * pos[0:1], -2.0 * pos[1:2], -2.0 * pos[2:3], high, middle, low, one, one, one)):
+        rows = jnp.broadcast_to(v * SCALE, (LEAVES, v.shape[1]))
+        target_feat[f * LEAVES : (f + 1) * LEAVES, :] = rows.astype(bf)
 
     for i in range(4, 8):
         fetch(i).wait()
@@ -348,16 +341,17 @@
         h = (y + (GRP - rel)) % GRP
         rows = place[rel][...].astype(f32)
         px, py, pz = rows[0:16], rows[16:32], rows[32:48]
+        ones = jnp.ones_like(px)
         parts = pieces(px * px + py * py + pz * pz)
-        for f, v in zip((0, 1, 2, 6, 7, 8), (px, py, pz) + parts):
-            source_feat[:, f, :] = v
+        pad = jnp.zeros((LANES - FEATS * LEAVES, BS), f32)
+        feats = jnp.concatenate((px, py, pz, ones, ones, ones) + parts + (pad,), axis=0)
+        feats = feats.T
+        lane_leaf = lax.broadcasted_iota(jnp.int32, feats.shape, 1) % LEAVES
         for c in range(CAP):
             at = wanted[h, c]
-            cols = slice(c * BS, (c + 1) * BS)
-            charge_sel[:, cols] = chunk[rel][at]
-            feat_sel[:, cols] = source_feat[at]
-        feat_sel_t[...] = feat_sel[...].T.astype(bf)
-        width, depth = 1024, 512
+            charge_sel[:, c * BS : (c + 1) * BS] = chunk[rel][at]
+            feat_sel[c * BS : (c + 1) * BS, :] = jnp.where(lane_leaf == at, feats, 0.0).astype(bf)
+        width, depth = 2048, 256
 
         def block(i, carry):
             cols = pl.ds(pl.multiple_of(i * width, width), width)
@@ -365,7 +359,7 @@
             w = weight[h, :, cols].astype(bf)
             total = None
             for k in range(0, CAP * BS, depth):
-                dist = dot(feat_sel_t[k : k + depth, :], targets)
+                dist = dot(feat_sel[k : k + depth, :], targets)
                 g = lax.rsqrt(dist.astype(bf))
                 g = jnp.concatenate(
                     [
@@ -437,7 +431,6 @@
     for k in range(1, X):
         x_copy(k, x).start()
     near(3)
-    near(5)
 
     for k in range(1, X):
         x_copy(k, (x + (X - k)) % X).wait_recv()
@@ -466,6 +459,7 @@
     for k in range(1, GRP):
         down_copy(k).start()
 
+    near(5)
     arrived(3, 0, left=False)
     arrived(3, 1, right=False)
     near(4)
@@ -532,10 +526,8 @@
             + [pltpu.VMEM((3 * LEAVES, BS), bf)] * 8
             + [
                 pltpu.VMEM((3 * LEAVES, BS), f32),
-                pltpu.VMEM((FEATS, points), bf),
-                pltpu.VMEM((LEAVES, FEATS, BS), f32),
-                pltpu.VMEM((FEATS, CAP * BS), f32),
-                pltpu.VMEM((CAP * BS, FEATS), bf),
+                pltpu.VMEM((LANES, points), bf),
+                pltpu.VMEM((CAP * BS, LANES), bf),
                 pltpu.VMEM((rows, CAP * BS), bf),
                 pltpu.VMEM((GRP, CAP, points), f32),
                 pltpu.VMEM((rows, points), f32),

time: 51.8 us -> 49.9 us (0.963)
  the two profiles are of different devices: /device:TPU:8 before, /device:TPU:1 now
where the time goes in v5:
time: 49.9 us; the launch traced here: 48.9 us
  Pallas kernels  47.2 us (95%)
  local copies, waits for them, and re-layouts  1.67 us (3%)
    pallas_call x1, Pallas kernels, shards(): pl.pallas_call(functools.partial(kernel, dims), out_shape=jax.ShapeDtypeS...  47.2 us
    unnamed x1, local copies, waits for them, and re-layouts  1.67 us

profile of v5, /device:TPU:1, one launch (start us, length us, event | category | flops | bytes accessed | tf_op | source)
XLA Modules:
  0.0 48.9 jit_solution(16666731475878066522)
XLA Ops:
  0.0 47.2 %shard_map.91 = bf16[64,2048]{1,0:T(8,128)(2,1)} custom-call(s32[8,8]{1,0:T(8,128)} %bitcast.7, s32[1,64]{1,0:T(1,128)} %far_source_in.1, bf16[64,2048]{1,0:T(8,128)(2,1)} %charges_in.1, bf16[3,2048]{1,0:T(4,128)(2,1)} %positions_in.1, bf16[64,2048]{1,0:T(8,128)(2,1)} %bases_in.1, bf16[16,64,64]{2,1,0:T(8,128)(2,1)} %transfers_in.1, ...), custom_call_target="tpu_custom_call" | custom-call | tf_op jit(solution)/shard_map/pallas_call | solution.py:509
  47.2 1.7 %copy.11 = bf16[64,2048]{1,0:T(8,128)(2,1)} copy(bf16[64,2048]{1,0:T(8,128)(2,1)} %shard_map.91) | data formatting | bytes 524288

commit v6 on v5

--- a/solution.py
+++ b/solution.py
@@ -392,6 +392,7 @@
                     ring(way, 3, half).start()
 
     near(0, first=True)
+    arrived(0, 0)
 
     for k in range(1, GRP):
         up_copy(k).wait_recv()
@@ -401,7 +402,6 @@
     if C > 1:
         sibling[0] = total.astype(bf)
         core_copy().start()
-    arrived(0, 0)
     if C > 1:
         core_copy().wait_recv()
         side = lax.broadcasted_iota(jnp.int32, total.shape, 1) // (total.shape[1] // 2)

time: 49.9 us -> 50.7 us (1.016); the launches traced: 48.9 us -> 50.5 us
  Pallas kernels: 47.2 us -> 48.8 us
    pallas_call x1, Pallas kernels: 47.2 us -> 48.8 us  [shards(): pl.pallas_call(functools.partial(kernel, dims), out_shape=jax.ShapeDtypeS...]
where the time goes in v6:
time: 50.7 us; the launch traced here: 50.5 us
  Pallas kernels  48.8 us (96%)
  local copies, waits for them, and re-layouts  1.67 us (3%)
    pallas_call x1, Pallas kernels, shards(): pl.pallas_call(functools.partial(kernel, dims), out_shape=jax.ShapeDtypeS...  48.8 us
    unnamed x1, local copies, waits for them, and re-layouts  1.67 us

profile of v6, /device:TPU:1, one launch (start us, length us, event | category | flops | bytes accessed | tf_op | source)
XLA Modules:
  0.0 50.5 jit_solution(12704028740322816554)
XLA Ops:
  0.0 48.8 %shard_map.91 = bf16[64,2048]{1,0:T(8,128)(2,1)} custom-call(s32[8,8]{1,0:T(8,128)} %bitcast.7, s32[1,64]{1,0:T(1,128)} %far_source_in.1, bf16[64,2048]{1,0:T(8,128)(2,1)} %charges_in.1, bf16[3,2048]{1,0:T(4,128)(2,1)} %positions_in.1, bf16[64,2048]{1,0:T(8,128)(2,1)} %bases_in.1, bf16[16,64,64]{2,1,0:T(8,128)(2,1)} %transfers_in.1, ...), custom_call_target="tpu_custom_call" | custom-call | tf_op jit(solution)/shard_map/pallas_call | solution.py:509
  48.8 1.7 %copy.11 = bf16[64,2048]{1,0:T(8,128)(2,1)} copy(bf16[64,2048]{1,0:T(8,128)(2,1)} %shard_map.91) | data formatting | bytes 524288
